TPU v7x, 128 devices: a whole 4x4x4 slice. The times are simulated.
128 devices in a mesh: gx: 4 (over z), gy: 4 (over x), gz: 8 (over y, core).
Axes of the slice: x: 4, y: 4, z: 4, core: 2. Of those that a mesh axis runs over, the one named last changes fastest.
Arguments:
- stencil: bfloat16 [7, 4, 32, 128, 2048], P(None, None, 'gx', 'gy', 'gz'), may hold values from -1.5 to 13, as said below
- right_side: float32 [2, 32, 128, 2048], P(None, 'gx', 'gy', 'gz'), may hold values from -25 to 25
Outputs:
- solution: float32 [2, 32, 128, 2048], P(None, 'gx', 'gy', 'gz')
- residual: float32 [2, 32, 128, 2048], P(None, 'gx', 'gy', 'gz')
Inputs may be any that keep to these rules, and one draw needn't show every extreme that they name: `stencil`: entries of the operator's blocks.
All inputs are finite; a program needn't handle non-finite values.
Results may differ from a plain program's by a relative error of at most 0.008.
Values may be sent and summed in bfloat16 or wider, within the bound.
A program may use at most 192 MiB of HBM per device.

v0:
```python
import functools

import jax
import jax.numpy as jnp
from jax import lax
from jax.experimental import pallas as pl
from jax.experimental.pallas import tpu as pltpu
from jax.sharding import PartitionSpec as P

MESH = pl.DeviceIdType.MESH
S = 4
AHEAD = 2
shifts = (15.0, 2.0, 8.5, 4.75)
scale = 6.5
inv = 1.0 / scale

NW = S + 1 + AHEAD
NV = NW + S + 1
PITCH = 40
LANES = 128


def row(x, lt):
    return (2 * x + lt) * PITCH + 8


def kernel(
    sizes, st_hbm, rs_hbm, sol_ref, res_ref,
    st, W, xC, yC, zC, yh, ys, zh, zs, gacc, ar1, ar2, gB, cf,
    load_sem, ssem, rsem, s1sem, r1sem, s2sem, r2sem,
):
    ngx, ngy, ngz = sizes
    gx, gy, gz = (lax.axis_index(a) for a in ("gx", "gy", "gz"))
    NX, NY = 8, 32
    have = (gx > 0, gx < ngx - 1, gy > 0, gy < ngy - 1, gz > 0, gz < ngz - 1)
    beside = (
        {"gx": lax.rem(gx + ngx - 1, ngx)}, {"gx": lax.rem(gx + 1, ngx)},
        {"gy": lax.rem(gy + ngy - 1, ngy)}, {"gy": lax.rem(gy + 1, ngy)},
        {"gz": lax.rem(gz + ngz - 1, ngz)}, {"gz": lax.rem(gz + 1, ngz)},
    )
    line = [{"gz": lax.rem(gz + k, ngz)} for k in range(1, ngz)]
    plane = [
        {"gx": lax.rem(gx + k // ngy, ngx), "gy": lax.rem(gy + k % ngy, ngy)}
        for k in range(1, ngx * ngy)
    ]
    lane = lax.broadcasted_iota(jnp.int32, (NY, LANES), 1)
    zero = jnp.zeros((NY, LANES), jnp.float32)

    loads = [pltpu.make_async_copy(st_hbm, st, load_sem.at[0])]
    for lt in range(2):
        for x in range(NX):
            loads.append(
                pltpu.make_async_copy(
                    rs_hbm.at[:, x, :, pl.ds(lt * LANES, LANES)],
                    W.at[0, :, pl.ds(row(x + 1, lt), NY), :],
                    load_sem.at[1 + lt * NX + x],
                )
            )
    for copy in loads[1:]:
        copy.start()
    loads[0].start()

    barrier = pltpu.get_barrier_semaphore()
    for peer in line + plane:
        pl.semaphore_signal(barrier, inc=1, device_id=peer, device_id_type=MESH)

    for v in range(NV):
        for c in range(2):
            for x in range(1, NX + 1):
                for lt in range(2):
                    W[v, c, pl.ds(row(x, lt) - 8, 8), :] = jnp.zeros((8, LANES), jnp.float32)
            W[v, c, pl.ds(row(NX + 1, 0) - 8, 8), :] = jnp.zeros((8, LANES), jnp.float32)
    for d in range(2):
        @pl.when(jnp.logical_not(have[d]))
        def _():
            for v in range(NV):
                for c in range(2):
                    for lt in range(2):
                        W[v, c, pl.ds(row(0 if d == 0 else NX + 1, lt), NY), :] = zero

        @pl.when(jnp.logical_not(have[2 + d]))
        def _():
            for v in range(NV):
                yh[v, d] = jnp.zeros((2, 2, NX, LANES), jnp.float32)

        @pl.when(jnp.logical_not(have[4 + d]))
        def _():
            for v in range(NV):
                zh[v, d] = zero
    for cyc in range(2):
        gacc[cyc, 15] = jnp.zeros((8, LANES), jnp.float32)

    def x_copy(v, side, lt):
        src = W.at[v, :, pl.ds(row(1 if side == 0 else NX, lt), NY), :]
        dst = W.at[v, :, pl.ds(row(NX + 1 if side == 0 else 0, lt), NY), :]
        k = 2 * side + lt
        return pltpu.make_async_remote_copy(
            src, dst, ssem.at[v, k], rsem.at[v, k], device_id=beside[side], device_id_type=MESH
        )

    def y_copy(v, side):
        k = 4 + side
        return pltpu.make_async_remote_copy(
            ys.at[v, side], yh.at[v, 1 - side], ssem.at[v, k], rsem.at[v, k],
            device_id=beside[2 + side], device_id_type=MESH,
        )

    def z_copy(v, side):
        k = 6 + side
        return pltpu.make_async_remote_copy(
            zs.at[v, side], zh.at[v, 1 - side], ssem.at[v, k], rsem.at[v, k],
            device_id=beside[4 + side], device_id_type=MESH,
        )

    def send_x(v, side, lt):
        @pl.when(have[side])
        def _():
            x_copy(v, side, lt).start()

    def pack_send(v):
        for side in range(2):
            for c in range(2):
                for lt in range(2):
                    ys[v, side, c, lt] = W[
                        v, c, pl.ds(row(1, lt) + (0 if side == 0 else NY - 1), NX, stride=2 * PITCH), :
                    ]

            @pl.when(have[2 + side])
            def _():
                y_copy(v, side).start()
        for side in range(2):
            packed = zero
            for c in range(2):
                for x in range(NX):
                    n = c * NX + x
                    tile = W[v, c, pl.ds(row(x + 1, side), NY), :]
                    turn = n if side == 0 else n + 1
                    if turn:
                        tile = pltpu.roll(tile, turn, 1)
                    packed = jnp.where(lane == n, tile, packed)
            zs[v, side] = packed

            @pl.when(have[4 + side])
            def _():
                z_copy(v, side).start()

    def wait_halo(copy, side, axis):
        @pl.when(have[2 * axis + side])
        def _():
            copy.wait_recv()

    def interior_plane(v, x, left, right, shift):
        out = v + 1
        acc = [[None, None], [None, None]]

        def add(lt, p, b, src):
            for a in range(2):
                term = st[p, 2 * a + b, x - 1, :, lt * LANES:(lt + 1) * LANES].astype(jnp.float32) * src
                acc[lt][a] = term if acc[lt][a] is None else acc[lt][a] + term

        def at(b, xx, lt, off=0):
            start = row(xx, lt)
            if off == 0 and not isinstance(start, int):
                start = pl.multiple_of(start, 8)
            return W[v, b, pl.ds(start + off, NY), :]

        for b in range(2):
            centre = [at(b, x, lt) for lt in range(2)]
            up = [pltpu.roll(t, 1, 1) for t in centre]
            down = [pltpu.roll(t, LANES - 1, 1) for t in centre]
            for lt in range(2):
                add(lt, 0, b, centre[lt])
            add(0, 5, b, jnp.where(lane == 0, 0.0, up[0]))
            add(1, 5, b, jnp.where(lane == 0, up[0], up[1]))
            add(0, 6, b, jnp.where(lane == LANES - 1, down[1], down[0]))
            add(1, 6, b, jnp.where(lane == LANES - 1, 0.0, down[1]))
            for lt in range(2):
                if left:
                    add(lt, 1, b, at(b, x - 1, lt))
                if right:
                    add(lt, 2, b, at(b, x + 1, lt))
                add(lt, 3, b, at(b, x, lt, -1))
                add(lt, 4, b, at(b, x, lt, 1))
        for lt in range(2):
            for a in range(2):
                start = row(x, lt)
                if not isinstance(start, int):
                    start = pl.multiple_of(start, 8)
                W[out, a, pl.ds(start, NY), :] = (acc[lt][a] - shift * at(a, x, lt)) * inv

    def interior(v, shift):
        interior_plane(v, 1, False, True, shift)

        def body(x, carry):
            interior_plane(v, x, True, True, shift)
            return carry

        lax.fori_loop(2, NX, body, 0)
        interior_plane(v, NX, True, False, shift)

    def fix_y(v):
        out = v + 1
        for side in range(2):
            for lt in range(2):
                h = [yh[v, side, b, lt] for b in range(2)]
                for a in range(2):
                    part = yC[side, 2 * a, lt] * h[0] + yC[side, 2 * a + 1, lt] * h[1]
                    rows = pl.ds(row(1, lt) + (0 if side == 0 else NY - 1), NX, stride=2 * PITCH)
                    W[out, a, rows, :] = W[out, a, rows, :] + part

    def fix_z(v):
        out = v + 1
        for side in range(2):
            h = zh[v, side]
            other = jnp.where(lane < NX, pltpu.roll(h, LANES - NX, 1), pltpu.roll(h, NX, 1))
            part = zC[side, 0] * h + zC[side, 1] * other
            edge = 0 if side == 0 else LANES - 1
            for a in range(2):
                for x in range(NX):
                    turn = (edge - (a * NX + x)) % LANES
                    moved = pltpu.roll(part, turn, 1) if turn else part
                    rows = pl.ds(row(x + 1, side), NY)
                    W[out, a, rows, :] = W[out, a, rows, :] + jnp.where(lane == edge, moved, 0.0)

    def fix_x(v, side, lt):
        out = v + 1
        src = row(0 if side == 0 else NX + 1, lt)
        dst = pl.ds(row(1 if side == 0 else NX, lt), NY)
        h = [W[v, b, pl.ds(src, NY), :] for b in range(2)]
        for a in range(2):
            part = xC[side, 2 * a, lt] * h[0] + xC[side, 2 * a + 1, lt] * h[1]
            W[out, a, dst, :] = W[out, a, dst, :] + part

    def finish(v, sent, local):
        if not local:
            for side in range(2):
                wait_halo(y_copy(v, 1 - side), side, 1)
                wait_halo(z_copy(v, 1 - side), side, 2)
        fix_y(v)
        fix_z(v)
        for lt in range(2):
            for side in range(2):
                if not local:
                    wait_halo(x_copy(v, 1 - side, lt), side, 0)
                fix_x(v, side, lt)
                if sent:
                    send_x(v + 1, side, lt)
        if sent:
            pack_send(v + 1)

    def gram_row(cyc, first, j):
        def body(x, accs):
            accs = list(accs)
            for c in range(2):
                for lt in range(2):
                    rows = pl.ds(pl.multiple_of(row(x, lt), 8), NY)
                    right = W[first + j, c, rows, :]
                    for i in range(j + 1):
                        left = right if i == j else W[first + i, c, rows, :]
                        accs[i] = accs[i] + jnp.sum((left * right).reshape(NY // 8, 8, LANES), axis=0)
            return tuple(accs)

        accs = lax.fori_loop(1, NX + 1, body, tuple(jnp.zeros((8, LANES), jnp.float32) for _ in range(j + 1)))
        for i in range(j + 1):
            gacc[cyc, j * (j + 1) // 2 + i] = accs[i]

    def line_copy(cyc, k):
        return pltpu.make_async_remote_copy(
            ar1.at[cyc, gz], ar1.at[cyc, gz], s1sem.at[cyc, k], r1sem.at[cyc, k],
            device_id=line[k], device_id_type=MESH,
        )

    def plane_copy(cyc, k):
        slot = gx * ngy + gy
        return pltpu.make_async_remote_copy(
            ar2.at[cyc, slot], ar2.at[cyc, slot], s2sem.at[cyc, k], r2sem.at[cyc, k],
            device_id=plane[k], device_id_type=MESH,
        )

    def reduce_start(cyc):
        ar1[cyc, gz] = jnp.sum(gacc[cyc], axis=1)
        for k in range(ngz - 1):
            line_copy(cyc, k).start()

    def reduce_middle(cyc):
        for k in range(ngz - 1):
            line_copy(cyc, k).wait_recv()
        ar2[cyc, gx * ngy + gy] = jnp.sum(ar1[cyc], axis=0)
        for k in range(ngx * ngy - 1):
            plane_copy(cyc, k).start()

    def reduce_end(cyc):
        for k in range(ngx * ngy - 1):
            plane_copy(cyc, k).wait_recv()
        total = jnp.sum(ar2[cyc], axis=0)
        gB[cyc] = jnp.broadcast_to(jnp.sum(total, axis=1, keepdims=True), (16, LANES))

    def solve(cyc):
        def G(i, j):
            i, j = min(i, j), max(i, j)
            return jnp.broadcast_to(gB[cyc, pl.ds(j * (j + 1) // 2 + i, 1), :], (8, LANES))

        g = [[G(i, j) for j in range(S + 1)] for i in range(S + 1)]
        gb = [[shifts[j] * g[i][j] + scale * g[i][j + 1] for j in range(S)] for i in range(S + 1)]
        h = [[shifts[i] * gb[i][j] + scale * gb[i + 1][j] if j <= i else None for j in range(S)] for i in range(S)]
        rhs = [gb[0][i] for i in range(S)]
        low = [[None] * S for _ in range(S)]
        dinv = [None] * S
        full = [[None] * S for _ in range(S)]
        for j in range(S):
            d = h[j][j]
            for k in range(j):
                d = d - low[j][k] * full[j][k]
            dinv[j] = 1.0 / d
            for i in range(j + 1, S):
                t = h[i][j]
                for k in range(j):
                    t = t - full[i][k] * low[j][k]
                full[i][j] = t
                low[i][j] = t * dinv[j]
        fwd = []
        for i in range(S):
            t = rhs[i]
            for k in range(i):
                t = t - low[i][k] * fwd[k]
            fwd.append(t)
        y = [None] * S
        for i in reversed(range(S)):
            t = fwd[i] * dinv[i]
            for k in range(i + 1, S):
                t = t - low[k][i] * y[k]
            y[i] = t
        c = []
        for j in range(S + 1):
            t = jnp.full((8, LANES), 1.0 if j == 0 else 0.0, jnp.float32)
            if j < S:
                t = t - shifts[j] * y[j]
            if j > 0:
                t = t - scale * y[j - 1]
            c.append(t)
        return y, c

    def put(n, value):
        cf[pl.ds(n, 1), :] = value[0:1]

    def coef(n):
        return cf[pl.ds(n, 1), :]

    for copy in loads[1:]:
        copy.wait()
    pl.semaphore_wait(barrier, ngz - 1 + ngx * ngy - 1)
    for lt in range(2):
        for side in range(2):
            send_x(0, side, lt)
    pack_send(0)
    loads[0].wait()

    for side in range(2):
        for e in range(4):
            for lt in range(2):
                lanes = slice(lt * LANES, (lt + 1) * LANES)
                xC[side, e, lt] = st[1 + side, e, 0 if side == 0 else NX - 1, :, lanes].astype(jnp.float32) * inv
                for x in range(NX):
                    part = st[3 + side, e, x, 16 * side:16 * side + 16, lanes].astype(jnp.float32) * inv
                    yC[side, e, lt, pl.ds(x, 1), :] = part[0:1] if side == 0 else part[15:16]
        lanes = slice(side * LANES, (side + 1) * LANES)
        for kind in range(2):
            packed = zero
            for c in range(2):
                e = 3 * c if kind == 0 else c + 1
                for x in range(NX):
                    n = c * NX + x
                    tile = st[5 + side, e, x, :, lanes].astype(jnp.float32) * inv
                    turn = n if side == 0 else n + 1
                    if turn:
                        tile = pltpu.roll(tile, turn, 1)
                    packed = jnp.where(lane == n, tile, packed)
            zC[side, kind] = packed

    for j in range(S + AHEAD):
        interior(j, shifts[j % S])
        if j < S:
            gram_row(0, 0, j)
        finish(j, True, False)
        if j + 1 == S:
            gram_row(0, 0, S)
            reduce_start(0)
        if j + 1 == S + 1:
            reduce_middle(0)
    if AHEAD == 0:
        reduce_middle(0)
    reduce_end(0)
    y, c = solve(0)
    for k in range(S):
        put(k, y[k])
    combo = [c + [None] * AHEAD]
    for j in range(AHEAD):
        old, new = combo[-1], []
        for k in range(NW):
            t = old[k - 1] if k > 0 else None
            factor = (shifts[k % S] - shifts[j]) * inv
            if old[k] is not None and factor != 0.0:
                t = factor * old[k] if t is None else t + factor * old[k]
            new.append(t)
        combo.append(new)
    place = {}
    for j in range(AHEAD + 1):
        for k in range(NW):
            if combo[j][k] is not None:
                place[j, k] = 8 + j * 8 + k
                put(place[j, k], combo[j][k])

    def combine(j, get):
        t = None
        for k in range(NW):
            if (j, k) in place:
                term = coef(place[j, k]) * get(k)
                t = term if t is None else t + term
        return t

    def second(x, carry):
        for cc in range(2):
            for lt in range(2):
                rows = pl.ds(pl.multiple_of(row(x, lt), 8), NY)
                tiles = [W[k, cc, rows, :] for k in range(NW)]
                for j in range(AHEAD + 1):
                    W[NW + j, cc, rows, :] = combine(j, lambda k: tiles[k])
        return carry

    lax.fori_loop(1, NX + 1, second, 0)
    last = NW + AHEAD
    interior(last, shifts[AHEAD])
    for side in range(2):
        wait_halo(y_copy(NW - 1, 1 - side), side, 1)
        wait_halo(z_copy(NW - 1, 1 - side), side, 2)
        for lt in range(2):
            wait_halo(x_copy(NW - 1, 1 - side, lt), side, 0)
    for side in range(2):
        for cc in range(2):
            for lt in range(2):
                rows = pl.ds(row(0 if side == 0 else NX + 1, lt), NY)
                W[last, cc, rows, :] = combine(AHEAD, lambda k: W[k, cc, rows, :])
                yh[last, side, cc, lt] = combine(AHEAD, lambda k: yh[k, side, cc, lt])
        zh[last, side] = combine(AHEAD, lambda k: zh[k, side])
    finish(last, True, True)
    for j in range(AHEAD + 1):
        gram_row(1, NW, j)

    for j in range(AHEAD + 1, S):
        v = NW + j
        interior(v, shifts[j])
        gram_row(1, NW, j)
        finish(v, j + 1 < S, False)
    gram_row(1, NW, S)
    reduce_start(1)

    def first_share(x, carry):
        for cc in range(2):
            for lt in range(2):
                rows = pl.ds(pl.multiple_of(row(x, lt), 8), NY)
                t = coef(0) * W[0, cc, rows, :]
                for k in range(1, S):
                    t = t + coef(k) * W[k, cc, rows, :]
                sol_ref[cc, x - 1, :, lt * LANES:(lt + 1) * LANES] = t
        return carry

    lax.fori_loop(1, NX + 1, first_share, 0)
    reduce_middle(1)
    reduce_end(1)
    y, c = solve(1)
    for k in range(S):
        put(k, y[k])
    for k in range(S + 1):
        put(8 + k, c[k])

    def final(x, carry):
        for cc in range(2):
            for lt in range(2):
                rows = pl.ds(pl.multiple_of(row(x, lt), 8), NY)
                lanes = slice(lt * LANES, (lt + 1) * LANES)
                tile = W[NW, cc, rows, :]
                s = sol_ref[cc, x - 1, :, lanes] + coef(0) * tile
                r = coef(8) * tile
                for k in range(1, S + 1):
                    tile = W[NW + k, cc, rows, :]
                    if k < S:
                        s = s + coef(k) * tile
                    r = r + coef(8 + k) * tile
                sol_ref[cc, x - 1, :, lanes] = s
                res_ref[cc, x - 1, :, lanes] = r
        return carry

    lax.fori_loop(1, NX + 1, final, 0)

    for v in list(range(NW)) + list(range(last + 1, NW + S)):
        for side in range(2):
            @pl.when(have[side])
            def _():
                for lt in range(2):
                    x_copy(v, side, lt).wait_send()

            @pl.when(have[2 + side])
            def _():
                y_copy(v, side).wait_send()

            @pl.when(have[4 + side])
            def _():
                z_copy(v, side).wait_send()
    for cyc in range(2):
        for k in range(ngz - 1):
            line_copy(cyc, k).wait_send()
        for k in range(ngx * ngy - 1):
            plane_copy(cyc, k).wait_send()


def solution(mesh):
    sizes = tuple(mesh.shape[a] for a in ("gx", "gy", "gz"))
    ngx, ngy, ngz = sizes

    def on_device(stencil, right_side):
        f32 = jnp.float32
        out = jax.ShapeDtypeStruct(right_side.shape, f32)
        dma = pltpu.SemaphoreType.DMA
        return pl.pallas_call(
            functools.partial(kernel, sizes),
            out_shape=(out, out),
            in_specs=[pl.BlockSpec(memory_space=pl.ANY)] * 2,
            out_specs=(pl.BlockSpec(memory_space=pltpu.VMEM),) * 2,
            scratch_shapes=[
                pltpu.VMEM(stencil.shape, stencil.dtype),
                pltpu.VMEM((NV, 2, 20 * PITCH + 8, LANES), f32),
                pltpu.VMEM((2, 4, 2, 32, LANES), f32),
                pltpu.VMEM((2, 4, 2, 8, LANES), f32),
                pltpu.VMEM((2, 2, 32, LANES), f32),
                pltpu.VMEM((NV, 2, 2, 2, 8, LANES), f32),
                pltpu.VMEM((NV, 2, 2, 2, 8, LANES), f32),
                pltpu.VMEM((NV, 2, 32, LANES), f32),
                pltpu.VMEM((NV, 2, 32, LANES), f32),
                pltpu.VMEM((2, 16, 8, LANES), f32),
                pltpu.VMEM((2, ngz, 16, LANES), f32),
                pltpu.VMEM((2, ngx * ngy, 16, LANES), f32),
                pltpu.VMEM((2, 16, LANES), f32),
                pltpu.VMEM((40, LANES), f32),
                dma((17,)),
                dma((NV, 8)),
                dma((NV, 8)),
                dma((2, ngz - 1)),
                dma((2, ngz - 1)),
                dma((2, ngx * ngy - 1)),
                dma((2, ngx * ngy - 1)),
            ],
            compiler_params=pltpu.CompilerParams(
                collective_id=0, has_side_effects=True, vmem_limit_bytes=48 << 20
            ),
            name="gmres",
        )(stencil, right_side)

    specs = (P(None, None, "gx", "gy", "gz"), P(None, "gx", "gy", "gz"))
    return jax.shard_map(
        on_device, mesh=mesh, in_specs=specs, out_specs=(specs[1], specs[1]), check_vma=False
    )
```

profile of v0, /device:TPU:1, one launch (start us, length us, event | category | flops | bytes accessed | tf_op | source)
XLA Modules:
  0.0 54.0 jit_solution(12931038804012097927)
XLA Ops:
  0.6 0.0 copy-start
  0.6 2.0 %copy-done = bf16[7,4,8,32,256]{4,3,2,1,0:T(8,128)(2,1)S(1)} copy-done((bf16[7,4,8,32,256]{4,3,2,1,0:T(8,128)(2,1)S(1)}, bf16[7,4,8,32,256]{4,3,2,1,0:T(8,128)(2,1)}, u32[]{:S(2)}) %copy-start) | copy-done | bytes 3670040
  2.7 0.0 copy-start.1
  2.7 1.0 %copy-done.1 = f32[2,8,32,256]{3,2,1,0:T(8,128)S(1)} copy-done((f32[2,8,32,256]{3,2,1,0:T(8,128)S(1)}, f32[2,8,32,256]{3,2,1,0:T(8,128)}, u32[]{:S(2)}) %copy-start.1) | copy-done | bytes 524312
  3.7 48.7 %gmres.1 = (f32[2,8,32,256]{3,2,1,0:T(8,128)S(1)}, f32[2,8,32,256]{3,2,1,0:T(8,128)S(1)}) custom-call(bf16[7,4,8,32,256]{4,3,2,1,0:T(8,128)(2,1)S(1)} %copy-done, f32[2,8,32,256]{3,2,1,0:T(8,128)S(1)} %copy-done.1), custom_call_target="tpu_custom_call" | custom-call | tf_op jit(solution)/shard_map/gmres/pallas_call | solution.py:524
  52.4 0.8 %copy.6 = f32[2,8,32,256]{3,2,1,0:T(8,128)} copy(f32[2,8,32,256]{3,2,1,0:T(8,128)S(1)} %get-tuple-element.4) | data formatting | bytes 1048576
  53.2 0.8 %copy.7 = f32[2,8,32,256]{3,2,1,0:T(8,128)} copy(f32[2,8,32,256]{3,2,1,0:T(8,128)S(1)} %get-tuple-element.5) | data formatting | bytes 1048576
Async XLA Ops:
  0.6 2.0 %copy-start = (bf16[7,4,8,32,256]{4,3,2,1,0:T(8,128)(2,1)S(1)}, bf16[7,4,8,32,256]{4,3,2,1,0:T(8,128)(2,1)}, u32[]{:S(2)}) copy-start(bf16[7,4,8,32,256]{4,3,2,1,0:T(8,128)(2,1)} %st_hbm.1) | copy-start | bytes 11010052
  2.7 1.0 %copy-start.1 = (f32[2,8,32,256]{3,2,1,0:T(8,128)S(1)}, f32[2,8,32,256]{3,2,1,0:T(8,128)}, u32[]{:S(2)}) copy-start(f32[2,8,32,256]{3,2,1,0:T(8,128)} %rs_hbm.1) | copy-start | bytes 1572868
where the time goes:
time: 54.2 us; the launch traced here: 54 us
  Pallas kernels  48.7 us (90%)
  local copies, waits for them, and re-layouts  4.66 us (9%)
  between operations  0.65 us (1%)
    pallas_call x1, Pallas kernels, on_device(): pl.pallas_call(functools.partial(kernel, sizes), out_shape=(out, out), in...  48.7 us
    unnamed x6, local copies, waits for them, and re-layouts  4.66 us

commit v1 on v0

--- a/solution.py
+++ b/solution.py
@@ -26,7 +26,7 @@
 
 def kernel(
     sizes, st_hbm, rs_hbm, sol_ref, res_ref,
-    st, W, xC, yC, zC, yh, ys, zh, zs, gacc, ar1, ar2, gB, cf,
+    st, W, xC, yC, eC, yh, ys, eh, eb, gacc, ar1, ar2, gB, cf,
     load_sem, ssem, rsem, s1sem, r1sem, s2sem, r2sem,
 ):
     ngx, ngy, ngz = sizes
@@ -44,6 +44,9 @@
         for k in range(1, ngx * ngy)
     ]
     lane = lax.broadcasted_iota(jnp.int32, (NY, LANES), 1)
+    lane8 = lax.broadcasted_iota(jnp.int32, (8, LANES), 1)
+    sub8 = lax.broadcasted_iota(jnp.int32, (8, LANES), 0)
+    eye = lax.broadcasted_iota(jnp.int32, (16, LANES), 1) == lax.broadcasted_iota(jnp.int32, (16, LANES), 0)
     zero = jnp.zeros((NY, LANES), jnp.float32)
 
     loads = [pltpu.make_async_copy(st_hbm, st, load_sem.at[0])]
@@ -83,10 +86,12 @@
             for v in range(NV):
                 yh[v, d] = jnp.zeros((2, 2, NX, LANES), jnp.float32)
 
-        @pl.when(jnp.logical_not(have[4 + d]))
+    for d in range(6):
+        @pl.when(jnp.logical_not(have[d]))
         def _():
             for v in range(NV):
-                zh[v, d] = zero
+                eh[v, d] = jnp.zeros((8, LANES), jnp.float32)
+
     for cyc in range(2):
         gacc[cyc, 15] = jnp.zeros((8, LANES), jnp.float32)
 
@@ -105,11 +110,10 @@
             device_id=beside[2 + side], device_id_type=MESH,
         )
 
-    def z_copy(v, side):
-        k = 6 + side
+    def e_copy(v, d):
         return pltpu.make_async_remote_copy(
-            zs.at[v, side], zh.at[v, 1 - side], ssem.at[v, k], rsem.at[v, k],
-            device_id=beside[4 + side], device_id_type=MESH,
+            eb.at[v], eh.at[v, d ^ 1], ssem.at[v, 6 + d], rsem.at[v, 6 + d],
+            device_id=beside[d], device_id_type=MESH,
         )
 
     def send_x(v, side, lt):
@@ -117,7 +121,7 @@
         def _():
             x_copy(v, side, lt).start()
 
-    def pack_send(v):
+    def send_y(v):
         for side in range(2):
             for c in range(2):
                 for lt in range(2):
@@ -128,26 +132,68 @@
             @pl.when(have[2 + side])
             def _():
                 y_copy(v, side).start()
+
+    def send_edges(v):
+        for d in range(6):
+            @pl.when(have[d])
+            def _():
+                e_copy(v, d).start()
+
+    def place_edge(packed, tile, side, t, c, x):
+        n = side * 64 + t * 16 + c * 8 + x
+        turn = n if side == 0 else (n + 1) % LANES
+        tile = tile[8 * t:8 * t + 8]
+        if turn:
+            tile = pltpu.roll(tile, turn, 1)
+        return jnp.where(lane8 == n, tile, packed)
+
+    def pack_edges(v):
+        packed = jnp.zeros((8, LANES), jnp.float32)
         for side in range(2):
-            packed = zero
             for c in range(2):
                 for x in range(NX):
-                    n = c * NX + x
                     tile = W[v, c, pl.ds(row(x + 1, side), NY), :]
-                    turn = n if side == 0 else n + 1
-                    if turn:
-                        tile = pltpu.roll(tile, turn, 1)
-                    packed = jnp.where(lane == n, tile, packed)
-            zs[v, side] = packed
-
-            @pl.when(have[4 + side])
-            def _():
-                z_copy(v, side).start()
+                    for t in range(4):
+                        packed = place_edge(packed, tile, side, t, c, x)
+        eb[v] = packed
+
+    def unpack_edges(v, planes):
+        packed = eb[v]
+        for side in range(2):
+            edge = 0 if side == 0 else LANES - 1
+            for c in range(2):
+                for x in planes:
+                    for t in range(4):
+                        turn = (edge - (side * 64 + t * 16 + c * 8 + x)) % LANES
+                        moved = pltpu.roll(packed, turn, 1) if turn else packed
+                        rows = pl.ds(row(x + 1, side) + 8 * t, 8)
+                        W[v, c, rows, :] = jnp.where(lane8 == edge, moved, W[v, c, rows, :])
+
+    def swapped(h):
+        return jnp.where((lane8 & 8) == 0, pltpu.roll(h, LANES - 8, 1), pltpu.roll(h, 8, 1))
+
+    def fix_edges(v):
+        hz = pltpu.roll(jnp.where(lane8 < 64, eh[v, 5], eh[v, 4]), 64, 1)
+        hy = jnp.where(
+            sub8 == 0,
+            pltpu.roll(pltpu.roll(eh[v, 2], LANES - 48, 1), 1, 0),
+            pltpu.roll(pltpu.roll(eh[v, 3], 48, 1), 7, 0),
+        )
+        hx = jnp.where((lane8 & 7) == 0, pltpu.roll(eh[v, 0], LANES - 7, 1), pltpu.roll(eh[v, 1], 7, 1))
+        part = eb[v + 1]
+        for axis, h in enumerate((hx, hy, hz)):
+            part = part + (eC[axis, 0] * h + eC[axis, 1] * swapped(h))
+        eb[v + 1] = part
 
     def wait_halo(copy, side, axis):
         @pl.when(have[2 * axis + side])
         def _():
             copy.wait_recv()
+
+    def wait_edges(v, d):
+        @pl.when(have[d])
+        def _():
+            e_copy(v, d ^ 1).wait_recv()
 
     def interior_plane(v, x, left, right, shift):
         out = v + 1
@@ -197,6 +243,7 @@
 
         lax.fori_loop(2, NX, body, 0)
         interior_plane(v, NX, True, False, shift)
+        pack_edges(v + 1)
 
     def fix_y(v):
         out = v + 1
@@ -207,20 +254,6 @@
                     part = yC[side, 2 * a, lt] * h[0] + yC[side, 2 * a + 1, lt] * h[1]
                     rows = pl.ds(row(1, lt) + (0 if side == 0 else NY - 1), NX, stride=2 * PITCH)
                     W[out, a, rows, :] = W[out, a, rows, :] + part
-
-    def fix_z(v):
-        out = v + 1
-        for side in range(2):
-            h = zh[v, side]
-            other = jnp.where(lane < NX, pltpu.roll(h, LANES - NX, 1), pltpu.roll(h, NX, 1))
-            part = zC[side, 0] * h + zC[side, 1] * other
-            edge = 0 if side == 0 else LANES - 1
-            for a in range(2):
-                for x in range(NX):
-                    turn = (edge - (a * NX + x)) % LANES
-                    moved = pltpu.roll(part, turn, 1) if turn else part
-                    rows = pl.ds(row(x + 1, side), NY)
-                    W[out, a, rows, :] = W[out, a, rows, :] + jnp.where(lane == edge, moved, 0.0)
 
     def fix_x(v, side, lt):
         out = v + 1
@@ -233,11 +266,16 @@
 
     def finish(v, sent, local):
         if not local:
+            for d in range(6):
+                wait_edges(v, d)
+        fix_edges(v)
+        if sent:
+            send_edges(v + 1)
+        unpack_edges(v + 1, (0, NX - 1))
+        if not local:
             for side in range(2):
                 wait_halo(y_copy(v, 1 - side), side, 1)
-                wait_halo(z_copy(v, 1 - side), side, 2)
         fix_y(v)
-        fix_z(v)
         for lt in range(2):
             for side in range(2):
                 if not local:
@@ -246,7 +284,8 @@
                 if sent:
                     send_x(v + 1, side, lt)
         if sent:
-            pack_send(v + 1)
+            send_y(v + 1)
+        unpack_edges(v + 1, range(1, NX - 1))
 
     def gram_row(cyc, first, j):
         def body(x, accs):
@@ -278,7 +317,8 @@
         )
 
     def reduce_start(cyc):
-        ar1[cyc, gz] = jnp.sum(gacc[cyc], axis=1)
+        rows = jnp.sum(jnp.sum(gacc[cyc], axis=1), axis=1, keepdims=True)
+        ar1[cyc, gz] = jnp.sum(jnp.where(eye, rows, 0.0), axis=0, keepdims=True)
         for k in range(ngz - 1):
             line_copy(cyc, k).start()
 
@@ -293,7 +333,8 @@
         for k in range(ngx * ngy - 1):
             plane_copy(cyc, k).wait_recv()
         total = jnp.sum(ar2[cyc], axis=0)
-        gB[cyc] = jnp.broadcast_to(jnp.sum(total, axis=1, keepdims=True), (16, LANES))
+        rows = jnp.sum(jnp.where(eye, total, 0.0), axis=1, keepdims=True)
+        gB[cyc] = jnp.broadcast_to(rows, (16, LANES))
 
     def solve(cyc):
         def G(i, j):
@@ -348,34 +389,49 @@
 
     for copy in loads[1:]:
         copy.wait()
+    pack_edges(0)
     pl.semaphore_wait(barrier, ngz - 1 + ngx * ngy - 1)
     for lt in range(2):
         for side in range(2):
             send_x(0, side, lt)
-    pack_send(0)
+    send_edges(0)
+    send_y(0)
     loads[0].wait()
+
+    def entry(p, e, x, lt):
+        return st[p, e, x, :, lt * LANES:(lt + 1) * LANES].astype(jnp.float32) * inv
 
     for side in range(2):
         for e in range(4):
             for lt in range(2):
-                lanes = slice(lt * LANES, (lt + 1) * LANES)
-                xC[side, e, lt] = st[1 + side, e, 0 if side == 0 else NX - 1, :, lanes].astype(jnp.float32) * inv
+                edge = 0 if lt == 0 else LANES - 1
+                xC[side, e, lt] = jnp.where(lane == edge, 0.0, entry(1 + side, e, 0 if side == 0 else NX - 1, lt))
                 for x in range(NX):
-                    part = st[3 + side, e, x, 16 * side:16 * side + 16, lanes].astype(jnp.float32) * inv
+                    part = st[3 + side, e, x, 16 * side:16 * side + 16, lt * LANES:(lt + 1) * LANES]
+                    part = jnp.where(lane[:16] == edge, 0.0, part.astype(jnp.float32) * inv)
                     yC[side, e, lt, pl.ds(x, 1), :] = part[0:1] if side == 0 else part[15:16]
-        lanes = slice(side * LANES, (side + 1) * LANES)
-        for kind in range(2):
-            packed = zero
+    for kind in range(2):
+        ex, ey, ez = (jnp.zeros((8, LANES), jnp.float32),) * 3
+        for side in range(2):
             for c in range(2):
                 e = 3 * c if kind == 0 else c + 1
                 for x in range(NX):
-                    n = c * NX + x
-                    tile = st[5 + side, e, x, :, lanes].astype(jnp.float32) * inv
-                    turn = n if side == 0 else n + 1
-                    if turn:
-                        tile = pltpu.roll(tile, turn, 1)
-                    packed = jnp.where(lane == n, tile, packed)
-            zC[side, kind] = packed
+                    tile = entry(5 + side, e, x, side)
+                    for t in range(4):
+                        ez = place_edge(ez, tile, side, t, c, x)
+                    ey = place_edge(ey, entry(3, e, x, side), side, 0, c, x)
+                    ey = place_edge(ey, entry(4, e, x, side), side, 3, c, x)
+                for p, x in ((1, 0), (2, NX - 1)):
+                    tile = entry(p, e, x, side)
+                    for t in range(4):
+                        ex = place_edge(ex, tile, side, t, c, x)
+        tile_y = (lane8 // 16) % 4
+        inside = jnp.logical_or(
+            jnp.logical_and(tile_y == 0, sub8 == 0), jnp.logical_and(tile_y == 3, sub8 == 7)
+        )
+        eC[0, kind] = ex
+        eC[1, kind] = jnp.where(inside, ey, 0.0)
+        eC[2, kind] = ez
 
     for j in range(S + AHEAD):
         interior(j, shifts[j % S])
@@ -432,16 +488,17 @@
     interior(last, shifts[AHEAD])
     for side in range(2):
         wait_halo(y_copy(NW - 1, 1 - side), side, 1)
-        wait_halo(z_copy(NW - 1, 1 - side), side, 2)
         for lt in range(2):
             wait_halo(x_copy(NW - 1, 1 - side, lt), side, 0)
+    for d in range(6):
+        wait_edges(NW - 1, d)
+        eh[last, d] = combine(AHEAD, lambda k: eh[k, d])
     for side in range(2):
         for cc in range(2):
             for lt in range(2):
                 rows = pl.ds(row(0 if side == 0 else NX + 1, lt), NY)
                 W[last, cc, rows, :] = combine(AHEAD, lambda k: W[k, cc, rows, :])
                 yh[last, side, cc, lt] = combine(AHEAD, lambda k: yh[k, side, cc, lt])
-        zh[last, side] = combine(AHEAD, lambda k: zh[k, side])
     finish(last, True, True)
     for j in range(AHEAD + 1):
         gram_row(1, NW, j)
@@ -503,9 +560,11 @@
             def _():
                 y_copy(v, side).wait_send()
 
-            @pl.when(have[4 + side])
+        for d in range(6):
+            @pl.when(have[d])
             def _():
-                z_copy(v, side).wait_send()
+                e_copy(v, d).wait_send()
+
     for cyc in range(2):
         for k in range(ngz - 1):
             line_copy(cyc, k).wait_send()
@@ -531,19 +590,19 @@
                 pltpu.VMEM((NV, 2, 20 * PITCH + 8, LANES), f32),
                 pltpu.VMEM((2, 4, 2, 32, LANES), f32),
                 pltpu.VMEM((2, 4, 2, 8, LANES), f32),
-                pltpu.VMEM((2, 2, 32, LANES), f32),
+                pltpu.VMEM((3, 2, 8, LANES), f32),
                 pltpu.VMEM((NV, 2, 2, 2, 8, LANES), f32),
                 pltpu.VMEM((NV, 2, 2, 2, 8, LANES), f32),
-                pltpu.VMEM((NV, 2, 32, LANES), f32),
-                pltpu.VMEM((NV, 2, 32, LANES), f32),
+                pltpu.VMEM((NV, 6, 8, LANES), f32),
+                pltpu.VMEM((NV, 8, LANES), f32),
                 pltpu.VMEM((2, 16, 8, LANES), f32),
-                pltpu.VMEM((2, ngz, 16, LANES), f32),
-                pltpu.VMEM((2, ngx * ngy, 16, LANES), f32),
+                pltpu.VMEM((2, ngz, 1, LANES), f32),
+                pltpu.VMEM((2, ngx * ngy, 1, LANES), f32),
                 pltpu.VMEM((2, 16, LANES), f32),
                 pltpu.VMEM((40, LANES), f32),
                 dma((17,)),
-                dma((NV, 8)),
-                dma((NV, 8)),
+                dma((NV, 12)),
+                dma((NV, 12)),
                 dma((2, ngz - 1)),
                 dma((2, ngz - 1)),
                 dma((2, ngx * ngy - 1)),
@@ -553,7 +612,10 @@
                 collective_id=0, has_side_effects=True, vmem_limit_bytes=48 << 20
             ),
             name="gmres",
-        )(stencil, right_side)
+        )(
+            pltpu.with_memory_space_constraint(stencil, pltpu.HBM),
+            pltpu.with_memory_space_constraint(right_side, pltpu.HBM),
+        )
 
     specs = (P(None, None, "gx", "gy", "gz"), P(None, "gx", "gy", "gz"))
     return jax.shard_map(

time: 54.2 us -> 50.9 us (0.939)
  local copies, waits for them, and re-layouts: 4.66 us -> 1.59 us
    unnamed x6 -> x2, local copies, waits for them, and re-layouts: 4.66 us -> 1.59 us
where the time goes in v1:
time: 50.9 us; the launch traced here: 50.7 us
  Pallas kernels  48.5 us (95%)
  local copies, waits for them, and re-layouts  1.59 us (3%)
  between operations  0.64 us (1%)
    pallas_call x1, Pallas kernels, on_device(): pl.pallas_call(functools.partial(kernel, sizes), out_shape=(out, out), in...  48.5 us
    unnamed x2, local copies, waits for them, and re-layouts  1.59 us

profile of v1, /device:TPU:1, one launch (start us, length us, event | category | flops | bytes accessed | tf_op | source)
XLA Modules:
  0.0 50.7 jit_solution(6303610711813773505)
XLA Ops:
  0.6 48.5 %gmres.1 = (f32[2,8,32,256]{3,2,1,0:T(8,128)S(1)}, f32[2,8,32,256]{3,2,1,0:T(8,128)S(1)}) custom-call(bf16[7,4,8,32,256]{4,3,2,1,0:T(8,128)(2,1)} %st_hbm.1, f32[2,8,32,256]{3,2,1,0:T(8,128)} %rs_hbm.1), custom_call_target="tpu_custom_call" | custom-call | tf_op jit(solution)/shard_map/gmres/pallas_call | solution.py:583
  49.1 0.8 %copy.6 = f32[2,8,32,256]{3,2,1,0:T(8,128)} copy(f32[2,8,32,256]{3,2,1,0:T(8,128)S(1)} %get-tuple-element.4) | data formatting | bytes 1048576
  49.9 0.8 %copy.7 = f32[2,8,32,256]{3,2,1,0:T(8,128)} copy(f32[2,8,32,256]{3,2,1,0:T(8,128)S(1)} %get-tuple-element.5) | data formatting | bytes 1048576

commit v2 on v1

--- a/solution.py
+++ b/solution.py
@@ -9,7 +9,7 @@
 
 MESH = pl.DeviceIdType.MESH
 S = 4
-AHEAD = 2
+AHEAD = 3
 shifts = (15.0, 2.0, 8.5, 4.75)
 scale = 6.5
 inv = 1.0 / scale
@@ -27,7 +27,7 @@
 def kernel(
     sizes, st_hbm, rs_hbm, sol_ref, res_ref,
     st, W, xC, yC, eC, yh, ys, eh, eb, gacc, ar1, ar2, gB, cf,
-    load_sem, ssem, rsem, s1sem, r1sem, s2sem, r2sem,
+    load_sem, near_sem, ssem, rsem, s1sem, r1sem, s2sem, r2sem,
 ):
     ngx, ngy, ngz = sizes
     gx, gy, gz = (lax.axis_index(a) for a in ("gx", "gy", "gz"))
@@ -64,7 +64,7 @@
     loads[0].start()
 
     barrier = pltpu.get_barrier_semaphore()
-    for peer in line + plane:
+    for peer in beside:
         pl.semaphore_signal(barrier, inc=1, device_id=peer, device_id_type=MESH)
 
     for v in range(NV):
@@ -95,6 +95,10 @@
     for cyc in range(2):
         gacc[cyc, 15] = jnp.zeros((8, LANES), jnp.float32)
 
+    def tell(step):
+        for peer in beside:
+            pl.semaphore_signal(near_sem.at[step], inc=1, device_id=peer, device_id_type=MESH)
+
     def x_copy(v, side, lt):
         src = W.at[v, :, pl.ds(row(1 if side == 0 else NX, lt), NY), :]
         dst = W.at[v, :, pl.ds(row(NX + 1 if side == 0 else 0, lt), NY), :]
@@ -103,16 +107,16 @@
             src, dst, ssem.at[v, k], rsem.at[v, k], device_id=beside[side], device_id_type=MESH
         )
 
-    def y_copy(v, side):
-        k = 4 + side
+    def y_copy(v, side, lt):
+        k = 10 + 2 * side + lt
         return pltpu.make_async_remote_copy(
-            ys.at[v, side], yh.at[v, 1 - side], ssem.at[v, k], rsem.at[v, k],
+            ys.at[v, side, lt], yh.at[v, 1 - side, lt], ssem.at[v, k], rsem.at[v, k],
             device_id=beside[2 + side], device_id_type=MESH,
         )
 
     def e_copy(v, d):
         return pltpu.make_async_remote_copy(
-            eb.at[v], eh.at[v, d ^ 1], ssem.at[v, 6 + d], rsem.at[v, 6 + d],
+            eb.at[v], eh.at[v, d ^ 1], ssem.at[v, 4 + d], rsem.at[v, 4 + d],
             device_id=beside[d], device_id_type=MESH,
         )
 
@@ -121,17 +125,15 @@
         def _():
             x_copy(v, side, lt).start()
 
-    def send_y(v):
+    def send_y(v, lt):
         for side in range(2):
-            for c in range(2):
-                for lt in range(2):
-                    ys[v, side, c, lt] = W[
+            @pl.when(have[2 + side])
+            def _():
+                for c in range(2):
+                    ys[v, side, lt, c] = W[
                         v, c, pl.ds(row(1, lt) + (0 if side == 0 else NY - 1), NX, stride=2 * PITCH), :
                     ]
-
-            @pl.when(have[2 + side])
-            def _():
-                y_copy(v, side).start()
+                y_copy(v, side, lt).start()
 
     def send_edges(v):
         for d in range(6):
@@ -245,15 +247,13 @@
         interior_plane(v, NX, True, False, shift)
         pack_edges(v + 1)
 
-    def fix_y(v):
+    def fix_y(v, side, lt):
         out = v + 1
-        for side in range(2):
-            for lt in range(2):
-                h = [yh[v, side, b, lt] for b in range(2)]
-                for a in range(2):
-                    part = yC[side, 2 * a, lt] * h[0] + yC[side, 2 * a + 1, lt] * h[1]
-                    rows = pl.ds(row(1, lt) + (0 if side == 0 else NY - 1), NX, stride=2 * PITCH)
-                    W[out, a, rows, :] = W[out, a, rows, :] + part
+        h = [yh[v, side, lt, b] for b in range(2)]
+        for a in range(2):
+            part = yC[side, 2 * a, lt] * h[0] + yC[side, 2 * a + 1, lt] * h[1]
+            rows = pl.ds(row(1, lt) + (0 if side == 0 else NY - 1), NX, stride=2 * PITCH)
+            W[out, a, rows, :] = W[out, a, rows, :] + part
 
     def fix_x(v, side, lt):
         out = v + 1
@@ -272,20 +272,37 @@
         if sent:
             send_edges(v + 1)
         unpack_edges(v + 1, (0, NX - 1))
-        if not local:
-            for side in range(2):
-                wait_halo(y_copy(v, 1 - side), side, 1)
-        fix_y(v)
         for lt in range(2):
             for side in range(2):
-                if not local:
-                    wait_halo(x_copy(v, 1 - side, lt), side, 0)
-                fix_x(v, side, lt)
-                if sent:
-                    send_x(v + 1, side, lt)
-        if sent:
-            send_y(v + 1)
+                @pl.when(have[2 + side])
+                def _():
+                    if not local:
+                        y_copy(v, 1 - side, lt).wait_recv()
+                    fix_y(v, side, lt)
+
+            for side in range(2):
+                @pl.when(have[side])
+                def _():
+                    if not local:
+                        x_copy(v, 1 - side, lt).wait_recv()
+                    fix_x(v, side, lt)
+                    if sent:
+                        x_copy(v + 1, side, lt).start()
+            if sent:
+                send_y(v + 1, lt)
         unpack_edges(v + 1, range(1, NX - 1))
+
+    def drain(v):
+        for d in range(6):
+            @pl.when(have[d])
+            def _():
+                if d < 2:
+                    for lt in range(2):
+                        x_copy(v, d, lt).wait_send()
+                elif d < 4:
+                    for lt in range(2):
+                        y_copy(v, d - 2, lt).wait_send()
+                e_copy(v, d).wait_send()
 
     def gram_row(cyc, first, j):
         def body(x, accs):
@@ -390,12 +407,13 @@
     for copy in loads[1:]:
         copy.wait()
     pack_edges(0)
-    pl.semaphore_wait(barrier, ngz - 1 + ngx * ngy - 1)
+    pl.semaphore_wait(barrier, 6)
+    tell(0)
+    send_edges(0)
     for lt in range(2):
         for side in range(2):
             send_x(0, side, lt)
-    send_edges(0)
-    send_y(0)
+        send_y(0, lt)
     loads[0].wait()
 
     def entry(p, e, x, lt):
@@ -435,6 +453,12 @@
 
     for j in range(S + AHEAD):
         interior(j, shifts[j % S])
+        if j > 0:
+            drain(j - 1)
+        if j < 3:
+            pl.semaphore_wait(near_sem.at[j], 6)
+            if j < 2:
+                tell(j + 1)
         if j < S:
             gram_row(0, 0, j)
         finish(j, True, False)
@@ -486,9 +510,10 @@
     lax.fori_loop(1, NX + 1, second, 0)
     last = NW + AHEAD
     interior(last, shifts[AHEAD])
+    drain(NW - 2)
     for side in range(2):
-        wait_halo(y_copy(NW - 1, 1 - side), side, 1)
         for lt in range(2):
+            wait_halo(y_copy(NW - 1, 1 - side, lt), side, 1)
             wait_halo(x_copy(NW - 1, 1 - side, lt), side, 0)
     for d in range(6):
         wait_edges(NW - 1, d)
@@ -498,8 +523,8 @@
             for lt in range(2):
                 rows = pl.ds(row(0 if side == 0 else NX + 1, lt), NY)
                 W[last, cc, rows, :] = combine(AHEAD, lambda k: W[k, cc, rows, :])
-                yh[last, side, cc, lt] = combine(AHEAD, lambda k: yh[k, side, cc, lt])
-    finish(last, True, True)
+                yh[last, side, lt, cc] = combine(AHEAD, lambda k: yh[k, side, lt, cc])
+    finish(last, AHEAD + 1 < S, True)
     for j in range(AHEAD + 1):
         gram_row(1, NW, j)
 
@@ -522,7 +547,16 @@
         return carry
 
     lax.fori_loop(1, NX + 1, first_share, 0)
+    drain(NW - 1)
+    for v in range(last + 1, NW + S):
+        drain(v)
+    for k in range(ngz - 1):
+        line_copy(0, k).wait_send()
+    for k in range(ngx * ngy - 1):
+        plane_copy(0, k).wait_send()
     reduce_middle(1)
+    for k in range(ngz - 1):
+        line_copy(1, k).wait_send()
     reduce_end(1)
     y, c = solve(1)
     for k in range(S):
@@ -548,28 +582,8 @@
         return carry
 
     lax.fori_loop(1, NX + 1, final, 0)
-
-    for v in list(range(NW)) + list(range(last + 1, NW + S)):
-        for side in range(2):
-            @pl.when(have[side])
-            def _():
-                for lt in range(2):
-                    x_copy(v, side, lt).wait_send()
-
-            @pl.when(have[2 + side])
-            def _():
-                y_copy(v, side).wait_send()
-
-        for d in range(6):
-            @pl.when(have[d])
-            def _():
-                e_copy(v, d).wait_send()
-
-    for cyc in range(2):
-        for k in range(ngz - 1):
-            line_copy(cyc, k).wait_send()
-        for k in range(ngx * ngy - 1):
-            plane_copy(cyc, k).wait_send()
+    for k in range(ngx * ngy - 1):
+        plane_copy(1, k).wait_send()
 
 
 def solution(mesh):
@@ -601,8 +615,9 @@
                 pltpu.VMEM((2, 16, LANES), f32),
                 pltpu.VMEM((40, LANES), f32),
                 dma((17,)),
-                dma((NV, 12)),
-                dma((NV, 12)),
+                pltpu.SemaphoreType.REGULAR((3,)),
+                dma((NV, 14)),
+                dma((NV, 14)),
                 dma((2, ngz - 1)),
                 dma((2, ngz - 1)),
                 dma((2, ngx * ngy - 1)),

time: 50.9 us -> 48.6 us (0.955)
  Pallas kernels: 48.5 us -> 46.1 us
    pallas_call x1, Pallas kernels: 48.5 us -> 46.1 us  [on_device(): pl.pallas_call(functools.partial(kernel, sizes), out_shape=(out, out), in...]
where the time goes in v2:
time: 48.6 us; the launch traced here: 48.3 us
  Pallas kernels  46.1 us (95%)
  local copies, waits for them, and re-layouts  1.59 us (3%)
  between operations  0.64 us (1%)
    pallas_call x1, Pallas kernels, on_device(): pl.pallas_call(functools.partial(kernel, sizes), out_shape=(out, out), in...  46.1 us
    unnamed x2, local copies, waits for them, and re-layouts  1.59 us

profile of v2, /device:TPU:1, one launch (start us, length us, event | category | flops | bytes accessed | tf_op | source)
XLA Modules:
  0.0 48.3 jit_solution(14435278469724674508)
XLA Ops:
  0.6 46.1 %gmres.1 = (f32[2,8,32,256]{3,2,1,0:T(8,128)S(1)}, f32[2,8,32,256]{3,2,1,0:T(8,128)S(1)}) custom-call(bf16[7,4,8,32,256]{4,3,2,1,0:T(8,128)(2,1)} %st_hbm.1, f32[2,8,32,256]{3,2,1,0:T(8,128)} %rs_hbm.1), custom_call_target="tpu_custom_call" | custom-call | tf_op jit(solution)/shard_map/gmres/pallas_call | solution.py:597
  46.7 0.8 %copy.6 = f32[2,8,32,256]{3,2,1,0:T(8,128)} copy(f32[2,8,32,256]{3,2,1,0:T(8,128)S(1)} %get-tuple-element.4) | data formatting | bytes 1048576
  47.5 0.8 %copy.7 = f32[2,8,32,256]{3,2,1,0:T(8,128)} copy(f32[2,8,32,256]{3,2,1,0:T(8,128)S(1)} %get-tuple-element.5) | data formatting | bytes 1048576

commit v3 on v2

--- a/solution.py
+++ b/solution.py
@@ -510,6 +510,8 @@
     lax.fori_loop(1, NX + 1, second, 0)
     last = NW + AHEAD
     interior(last, shifts[AHEAD])
+    for j in range(AHEAD + 1):
+        gram_row(1, NW, j)
     drain(NW - 2)
     for side in range(2):
         for lt in range(2):
@@ -525,8 +527,6 @@
                 W[last, cc, rows, :] = combine(AHEAD, lambda k: W[k, cc, rows, :])
                 yh[last, side, lt, cc] = combine(AHEAD, lambda k: yh[k, side, lt, cc])
     finish(last, AHEAD + 1 < S, True)
-    for j in range(AHEAD + 1):
-        gram_row(1, NW, j)
 
     for j in range(AHEAD + 1, S):
         v = NW + j
@@ -586,6 +586,18 @@
         plane_copy(1, k).wait_send()
 
 
+def store(sol_ref, res_ref, sol_hbm, res_hbm, sem):
+    copies = [
+        pltpu.make_async_copy(src.at[c], dst.at[c], sem.at[i, c])
+        for i, (src, dst) in enumerate(((sol_ref, sol_hbm), (res_ref, res_hbm)))
+        for c in range(2)
+    ]
+    for copy in copies:
+        copy.start()
+    for copy in copies:
+        copy.wait()
+
+
 def solution(mesh):
     sizes = tuple(mesh.shape[a] for a in ("gx", "gy", "gz"))
     ngx, ngy, ngz = sizes
@@ -594,7 +606,7 @@
         f32 = jnp.float32
         out = jax.ShapeDtypeStruct(right_side.shape, f32)
         dma = pltpu.SemaphoreType.DMA
-        return pl.pallas_call(
+        results = pl.pallas_call(
             functools.partial(kernel, sizes),
             out_shape=(out, out),
             in_specs=[pl.BlockSpec(memory_space=pl.ANY)] * 2,
@@ -631,6 +643,16 @@
             pltpu.with_memory_space_constraint(stencil, pltpu.HBM),
             pltpu.with_memory_space_constraint(right_side, pltpu.HBM),
         )
+        results = [pltpu.with_memory_space_constraint(r, pltpu.VMEM) for r in results]
+        return pl.pallas_call(
+            store,
+            out_shape=(out, out),
+            in_specs=[pl.BlockSpec(memory_space=pltpu.VMEM)] * 2,
+            out_specs=(pl.BlockSpec(memory_space=pl.ANY),) * 2,
+            scratch_shapes=[dma((2, 2))],
+            compiler_params=pltpu.CompilerParams(vmem_limit_bytes=4 << 20),
+            name="store",
+        )(*results)
 
     specs = (P(None, None, "gx", "gy", "gz"), P(None, "gx", "gy", "gz"))
     return jax.shard_map(

time: 48.6 us -> 47.4 us (0.975)
  local copies, waits for them, and re-layouts: 1.59 us -> 0 us
  Pallas kernels: 46.1 us -> 46.6 us
    unnamed x2 -> x0, local copies, waits for them, and re-layouts: 1.59 us -> none
    pallas_call x0 -> x1, Pallas kernels: none -> 1 us  [on_device(): pl.pallas_call(store, out_shape=(out, out), in_specs=[pl.BlockSpec(memory...]
    pallas_call x1, Pallas kernels: 46.1 us -> 45.6 us  [on_device(): pl.pallas_call(functools.partial(kernel, sizes), out_shape=(out, out), in...]
where the time goes in v3:
time: 47.4 us; the launch traced here: 47.2 us
  Pallas kernels  46.6 us (98%)
  between operations  0.64 us (1%)
    pallas_call x1, Pallas kernels, on_device(): pl.pallas_call(functools.partial(kernel, sizes), out_shape=(out, out), in...  45.6 us
    pallas_call x1, Pallas kernels, on_device(): pl.pallas_call(store, out_shape=(out, out), in_specs=[pl.BlockSpec(memory...  1 us

profile of v3, /device:TPU:1, one launch (start us, length us, event | category | flops | bytes accessed | tf_op | source)
XLA Modules:
  0.0 47.2 jit_solution(2612077799134522478)
XLA Ops:
  0.6 45.6 %gmres.1 = (f32[2,8,32,256]{3,2,1,0:T(8,128)S(1)}, f32[2,8,32,256]{3,2,1,0:T(8,128)S(1)}) custom-call(bf16[7,4,8,32,256]{4,3,2,1,0:T(8,128)(2,1)} %st_hbm.1, f32[2,8,32,256]{3,2,1,0:T(8,128)} %rs_hbm.1), custom_call_target="tpu_custom_call" | custom-call | tf_op jit(solution)/shard_map/gmres/pallas_call | solution.py:609
  46.2 1.0 %store.1 = (f32[2,8,32,256]{3,2,1,0:T(8,128)}, f32[2,8,32,256]{3,2,1,0:T(8,128)}) custom-call(f32[2,8,32,256]{3,2,1,0:T(8,128)S(1)} %get-tuple-element.4.sol_ref, f32[2,8,32,256]{3,2,1,0:T(8,128)S(1)} %get-tuple-element.5.res_ref), custom_call_target="tpu_custom_call" | custom-call | tf_op jit(solution)/shard_map/store/pallas_call | solution.py:647

commit v4 on v3

--- a/solution.py
+++ b/solution.py
@@ -9,7 +9,7 @@
 
 MESH = pl.DeviceIdType.MESH
 S = 4
-AHEAD = 3
+AHEAD = S - 1
 shifts = (15.0, 2.0, 8.5, 4.75)
 scale = 6.5
 inv = 1.0 / scale
@@ -271,7 +271,8 @@
         fix_edges(v)
         if sent:
             send_edges(v + 1)
-        unpack_edges(v + 1, (0, NX - 1))
+        if sent:
+            unpack_edges(v + 1, (0, NX - 1))
         for lt in range(2):
             for side in range(2):
                 @pl.when(have[2 + side])
@@ -290,7 +291,8 @@
                         x_copy(v + 1, side, lt).start()
             if sent:
                 send_y(v + 1, lt)
-        unpack_edges(v + 1, range(1, NX - 1))
+        if sent:
+            unpack_edges(v + 1, range(1, NX - 1))
 
     def drain(v):
         for d in range(6):
@@ -490,9 +492,9 @@
                 place[j, k] = 8 + j * 8 + k
                 put(place[j, k], combo[j][k])
 
-    def combine(j, get):
+    def combine(j, get, ks=range(NW)):
         t = None
-        for k in range(NW):
+        for k in ks:
             if (j, k) in place:
                 term = coef(place[j, k]) * get(k)
                 t = term if t is None else t + term
@@ -508,33 +510,47 @@
         return carry
 
     lax.fori_loop(1, NX + 1, second, 0)
+    for j in range(AHEAD + 1):
+        eb[NW + j] = combine(j, lambda k: eb[k])
     last = NW + AHEAD
     interior(last, shifts[AHEAD])
     for j in range(AHEAD + 1):
         gram_row(1, NW, j)
     drain(NW - 2)
+    early = range(NW - 1)
+    end = coef(place[AHEAD, NW - 1])
+    for side in range(2):
+        for cc in range(2):
+            for lt in range(2):
+                rows = pl.ds(row(0 if side == 0 else NX + 1, lt), NY)
+                W[last, cc, rows, :] = combine(AHEAD, lambda k: W[k, cc, rows, :], early)
+                yh[last, side, lt, cc] = combine(AHEAD, lambda k: yh[k, side, lt, cc], early)
+    for d in range(6):
+        eh[last, d] = combine(AHEAD, lambda k: eh[k, d], early)
     for side in range(2):
         for lt in range(2):
             wait_halo(y_copy(NW - 1, 1 - side, lt), side, 1)
             wait_halo(x_copy(NW - 1, 1 - side, lt), side, 0)
     for d in range(6):
         wait_edges(NW - 1, d)
-        eh[last, d] = combine(AHEAD, lambda k: eh[k, d])
+        eh[last, d] = eh[last, d] + end * eh[NW - 1, d]
     for side in range(2):
         for cc in range(2):
             for lt in range(2):
                 rows = pl.ds(row(0 if side == 0 else NX + 1, lt), NY)
-                W[last, cc, rows, :] = combine(AHEAD, lambda k: W[k, cc, rows, :])
-                yh[last, side, lt, cc] = combine(AHEAD, lambda k: yh[k, side, lt, cc])
-    finish(last, AHEAD + 1 < S, True)
-
-    for j in range(AHEAD + 1, S):
-        v = NW + j
-        interior(v, shifts[j])
-        gram_row(1, NW, j)
-        finish(v, j + 1 < S, False)
+                W[last, cc, rows, :] = W[last, cc, rows, :] + end * W[NW - 1, cc, rows, :]
+                yh[last, side, lt, cc] = yh[last, side, lt, cc] + end * yh[NW - 1, side, lt, cc]
+    edges_before = eb[last + 1]
+    finish(last, False, True)
+
     gram_row(1, NW, S)
+    edges = eb[last + 1]
+    base = S * (S + 1) // 2
+    for i in range(S):
+        gacc[1, base + i] = gacc[1, base + i] + eb[NW + i] * (edges - edges_before)
+    gacc[1, base + S] = gacc[1, base + S] + (edges * edges - edges_before * edges_before)
     reduce_start(1)
+    unpack_edges(last + 1, range(NX))
 
     def first_share(x, carry):
         for cc in range(2):

time: 47.4 us -> 47.1 us (level)
  no operation moved by 1% of the time
where the time goes in v4:
time: 47.1 us; the launch traced here: 46.9 us
  Pallas kernels  46.2 us (98%)
  between operations  0.64 us (1%)
    pallas_call x1, Pallas kernels, on_device(): pl.pallas_call(functools.partial(kernel, sizes), out_shape=(out, out), in...  45.2 us
    pallas_call x1, Pallas kernels, on_device(): pl.pallas_call(store, out_shape=(out, out), in_specs=[pl.BlockSpec(memory...  1 us

profile of v4, /device:TPU:1, one launch (start us, length us, event | category | flops | bytes accessed | tf_op | source)
XLA Modules:
  0.0 46.9 jit_solution(14205383214640938805)
XLA Ops:
  0.6 45.2 %gmres.1 = (f32[2,8,32,256]{3,2,1,0:T(8,128)S(1)}, f32[2,8,32,256]{3,2,1,0:T(8,128)S(1)}) custom-call(bf16[7,4,8,32,256]{4,3,2,1,0:T(8,128)(2,1)} %st_hbm.1, f32[2,8,32,256]{3,2,1,0:T(8,128)} %rs_hbm.1), custom_call_target="tpu_custom_call" | custom-call | tf_op jit(solution)/shard_map/gmres/pallas_call | solution.py:625
  45.9 1.0 %store.1 = (f32[2,8,32,256]{3,2,1,0:T(8,128)}, f32[2,8,32,256]{3,2,1,0:T(8,128)}) custom-call(f32[2,8,32,256]{3,2,1,0:T(8,128)S(1)} %get-tuple-element.4.sol_ref, f32[2,8,32,256]{3,2,1,0:T(8,128)S(1)} %get-tuple-element.5.res_ref), custom_call_target="tpu_custom_call" | custom-call | tf_op jit(solution)/shard_map/store/pallas_call | solution.py:663

commit v5 on v4

--- a/solution.py
+++ b/solution.py
@@ -25,7 +25,7 @@
 
 
 def kernel(
-    sizes, st_hbm, rs_hbm, sol_ref, res_ref,
+    sizes, st_hbm, rs_hbm, first_ref, basis_ref, weights_ref,
     st, W, xC, yC, eC, yh, ys, eh, eb, gacc, ar1, ar2, gB, cf,
     load_sem, near_sem, ssem, rsem, s1sem, r1sem, s2sem, r2sem,
 ):
@@ -559,7 +559,10 @@
                 t = coef(0) * W[0, cc, rows, :]
                 for k in range(1, S):
                     t = t + coef(k) * W[k, cc, rows, :]
-                sol_ref[cc, x - 1, :, lt * LANES:(lt + 1) * LANES] = t
+                lanes = slice(lt * LANES, (lt + 1) * LANES)
+                first_ref[cc, x - 1, :, lanes] = t
+                for k in range(S + 1):
+                    basis_ref[k, cc, x - 1, :, lanes] = W[NW + k, cc, rows, :]
         return carry
 
     lax.fori_loop(1, NX + 1, first_share, 0)
@@ -576,40 +579,34 @@
     reduce_end(1)
     y, c = solve(1)
     for k in range(S):
-        put(k, y[k])
+        weights_ref[k:k + 1, :] = y[k][0:1]
     for k in range(S + 1):
-        put(8 + k, c[k])
-
-    def final(x, carry):
-        for cc in range(2):
-            for lt in range(2):
-                rows = pl.ds(pl.multiple_of(row(x, lt), 8), NY)
-                lanes = slice(lt * LANES, (lt + 1) * LANES)
-                tile = W[NW, cc, rows, :]
-                s = sol_ref[cc, x - 1, :, lanes] + coef(0) * tile
-                r = coef(8) * tile
-                for k in range(1, S + 1):
-                    tile = W[NW + k, cc, rows, :]
-                    if k < S:
-                        s = s + coef(k) * tile
-                    r = r + coef(8 + k) * tile
-                sol_ref[cc, x - 1, :, lanes] = s
-                res_ref[cc, x - 1, :, lanes] = r
-        return carry
-
-    lax.fori_loop(1, NX + 1, final, 0)
+        weights_ref[8 + k:9 + k, :] = c[k][0:1]
     for k in range(ngx * ngy - 1):
         plane_copy(1, k).wait_send()
 
 
-def store(sol_ref, res_ref, sol_hbm, res_hbm, sem):
-    copies = [
-        pltpu.make_async_copy(src.at[c], dst.at[c], sem.at[i, c])
-        for i, (src, dst) in enumerate(((sol_ref, sol_hbm), (res_ref, res_hbm)))
-        for c in range(2)
-    ]
-    for copy in copies:
-        copy.start()
+def store(first_ref, basis_ref, weights_ref, sol_hbm, res_hbm, sol, res, sem):
+    copies = []
+    for x in range(sol.shape[1]):
+        for c in range(2):
+            for lt in range(2):
+                lanes = slice(lt * LANES, (lt + 1) * LANES)
+                s, r = first_ref[c, x, :, lanes], None
+                for k in range(S + 1):
+                    tile = basis_ref[k, c, x, :, lanes]
+                    if k < S:
+                        s = s + weights_ref[k:k + 1, :] * tile
+                    term = weights_ref[8 + k:9 + k, :] * tile
+                    r = term if r is None else r + term
+                sol[c, x, :, lanes] = s
+                res[c, x, :, lanes] = r
+        if x % 2 == 1:
+            planes = pl.ds(x - 1, 2)
+            for i, (src, dst) in enumerate(((sol, sol_hbm), (res, res_hbm))):
+                copy = pltpu.make_async_copy(src.at[:, planes], dst.at[:, planes], sem.at[i, x // 2])
+                copy.start()
+                copies.append(copy)
     for copy in copies:
         copy.wait()
 
@@ -624,9 +621,13 @@
         dma = pltpu.SemaphoreType.DMA
         results = pl.pallas_call(
             functools.partial(kernel, sizes),
-            out_shape=(out, out),
+            out_shape=(
+                out,
+                jax.ShapeDtypeStruct((S + 1,) + right_side.shape, f32),
+                jax.ShapeDtypeStruct((16, LANES), f32),
+            ),
             in_specs=[pl.BlockSpec(memory_space=pl.ANY)] * 2,
-            out_specs=(pl.BlockSpec(memory_space=pltpu.VMEM),) * 2,
+            out_specs=(pl.BlockSpec(memory_space=pltpu.VMEM),) * 3,
             scratch_shapes=[
                 pltpu.VMEM(stencil.shape, stencil.dtype),
                 pltpu.VMEM((NV, 2, 20 * PITCH + 8, LANES), f32),
@@ -663,9 +664,13 @@
         return pl.pallas_call(
             store,
             out_shape=(out, out),
-            in_specs=[pl.BlockSpec(memory_space=pltpu.VMEM)] * 2,
+            in_specs=[pl.BlockSpec(memory_space=pltpu.VMEM)] * 3,
             out_specs=(pl.BlockSpec(memory_space=pl.ANY),) * 2,
-            scratch_shapes=[dma((2, 2))],
+            scratch_shapes=[
+                pltpu.VMEM(right_side.shape, f32),
+                pltpu.VMEM(right_side.shape, f32),
+                dma((2, right_side.shape[1] // 2)),
+            ],
             compiler_params=pltpu.CompilerParams(vmem_limit_bytes=4 << 20),
             name="store",
         )(*results)

time: 47.1 us -> 46.9 us (level)
  no operation moved by 1% of the time
where the time goes in v5:
time: 46.9 us; the launch traced here: 46.6 us
  Pallas kernels  46 us (98%)
  between operations  0.64 us (1%)
    pallas_call x1, Pallas kernels, on_device(): pl.pallas_call(functools.partial(kernel, sizes), out_shape=(out, jax.Shap...  44.9 us
    pallas_call x1, Pallas kernels, on_device(): pl.pallas_call(store, out_shape=(out, out), in_specs=[pl.BlockSpec(memory...  1.07 us

profile of v5, /device:TPU:1, one launch (start us, length us, event | category | flops | bytes accessed | tf_op | source)
XLA Modules:
  0.0 46.6 jit_solution(14814787641016917428)
XLA Ops:
  0.6 44.9 %gmres.1 = (f32[2,8,32,256]{3,2,1,0:T(8,128)S(1)}, f32[5,2,8,32,256]{4,3,2,1,0:T(8,128)S(1)}, f32[16,128]{1,0:T(8,128)S(1)}) custom-call(bf16[7,4,8,32,256]{4,3,2,1,0:T(8,128)(2,1)} %st_hbm.1, f32[2,8,32,256]{3,2,1,0:T(8,128)} %rs_hbm.1), custom_call_target="tpu_custom_call" | custom-call | tf_op jit(solution)/shard_map/gmres/pallas_call | solution.py:622
  45.5 1.1 %store.1 = (f32[2,8,32,256]{3,2,1,0:T(8,128)}, f32[2,8,32,256]{3,2,1,0:T(8,128)}) custom-call(f32[2,8,32,256]{3,2,1,0:T(8,128)S(1)} %get-tuple-element.5.first_ref, f32[5,2,8,32,256]{4,3,2,1,0:T(8,128)S(1)} %get-tuple-element.6.basis_ref, f32[16,128]{1,0:T(8,128)S(1)} %get-tuple-element.7.weights_ref), custom_call_target="tpu_custom_call" | custom-call | tf_op jit(solution)/shard_map/store/pallas_call | solution.py:664

commit v6 on v5

--- a/solution.py
+++ b/solution.py
@@ -26,8 +26,8 @@
 
 def kernel(
     sizes, st_hbm, rs_hbm, first_ref, basis_ref, weights_ref,
-    st, W, xC, yC, eC, yh, ys, eh, eb, gacc, ar1, ar2, gB, cf,
-    load_sem, near_sem, ssem, rsem, s1sem, r1sem, s2sem, r2sem,
+    st, W, xC, yC, eC, yh, ys, eh, eb, gacc, ar1, ar2, pair, chips, gB, cf,
+    load_sem, near_sem, ssem, rsem, s1sem, r1sem, s2sem, r2sem, pair_sem, s3sem, r3sem,
 ):
     ngx, ngy, ngz = sizes
     gx, gy, gz = (lax.axis_index(a) for a in ("gx", "gy", "gz"))
@@ -322,38 +322,89 @@
         for i in range(j + 1):
             gacc[cyc, j * (j + 1) // 2 + i] = accs[i]
 
-    def line_copy(cyc, k):
+    def line_copy(k):
         return pltpu.make_async_remote_copy(
-            ar1.at[cyc, gz], ar1.at[cyc, gz], s1sem.at[cyc, k], r1sem.at[cyc, k],
-            device_id=line[k], device_id_type=MESH,
-        )
-
-    def plane_copy(cyc, k):
+            ar1.at[gz], ar1.at[gz], s1sem.at[k], r1sem.at[k], device_id=line[k], device_id_type=MESH
+        )
+
+    def plane_copy(k):
         slot = gx * ngy + gy
         return pltpu.make_async_remote_copy(
-            ar2.at[cyc, slot], ar2.at[cyc, slot], s2sem.at[cyc, k], r2sem.at[cyc, k],
-            device_id=plane[k], device_id_type=MESH,
-        )
-
-    def reduce_start(cyc):
+            ar2.at[slot], ar2.at[slot], s2sem.at[k], r2sem.at[k], device_id=plane[k], device_id_type=MESH
+        )
+
+    core = lax.rem(gz, 2)
+    nchip = ngz // 2
+    far = []
+    for k in range(1, ngx * ngy * nchip):
+        i, j, m = k // (ngy * nchip), k // nchip % ngy, k % nchip
+        far.append((-min(i, ngx - i) - min(j, ngy - j) - min(m, nchip - m), i, j, m))
+    far.sort()
+
+    def pair_copy():
+        return pltpu.make_async_remote_copy(
+            pair.at[core], pair.at[core], pair_sem.at[0], pair_sem.at[1],
+            device_id={"gz": gz + 1 - 2 * core}, device_id_type=MESH,
+        )
+
+    def chip_copy(k):
+        _, i, j, m = far[k]
+        slot = (gx * ngy + gy) * nchip + lax.div(gz, 2)
+        peer = {"gx": lax.rem(gx + i, ngx), "gy": lax.rem(gy + j, ngy), "gz": lax.rem(gz + 2 * m, ngz)}
+        return pltpu.make_async_remote_copy(
+            chips.at[slot], chips.at[slot], s3sem.at[k], r3sem.at[k], device_id=peer, device_id_type=MESH
+        )
+
+    def own_sums(cyc):
         rows = jnp.sum(jnp.sum(gacc[cyc], axis=1), axis=1, keepdims=True)
-        ar1[cyc, gz] = jnp.sum(jnp.where(eye, rows, 0.0), axis=0, keepdims=True)
-        for k in range(ngz - 1):
-            line_copy(cyc, k).start()
-
-    def reduce_middle(cyc):
-        for k in range(ngz - 1):
-            line_copy(cyc, k).wait_recv()
-        ar2[cyc, gx * ngy + gy] = jnp.sum(ar1[cyc], axis=0)
-        for k in range(ngx * ngy - 1):
-            plane_copy(cyc, k).start()
-
-    def reduce_end(cyc):
-        for k in range(ngx * ngy - 1):
-            plane_copy(cyc, k).wait_recv()
-        total = jnp.sum(ar2[cyc], axis=0)
+        return jnp.sum(jnp.where(eye, rows, 0.0), axis=0, keepdims=True)
+
+    def spread(cyc, total):
         rows = jnp.sum(jnp.where(eye, total, 0.0), axis=1, keepdims=True)
         gB[cyc] = jnp.broadcast_to(rows, (16, LANES))
+
+    def reduce_start(cyc):
+        if cyc == 0:
+            ar1[gz] = own_sums(0)
+            for k in range(ngz - 1):
+                line_copy(k).start()
+        else:
+            pair[core] = own_sums(1)
+            pair_copy().start()
+
+    def reduce_middle(cyc):
+        if cyc == 0:
+            for k in range(ngz - 1):
+                line_copy(k).wait_recv()
+            ar2[gx * ngy + gy] = jnp.sum(ar1[...], axis=0)
+            for k in range(ngx * ngy - 1):
+                plane_copy(k).start()
+        else:
+            pair_copy().wait_recv()
+            chips[(gx * ngy + gy) * nchip + lax.div(gz, 2)] = pair[0] + pair[1]
+            for k in range(len(far)):
+                chip_copy(k).start()
+
+    def reduce_end(cyc):
+        if cyc == 0:
+            for k in range(ngx * ngy - 1):
+                plane_copy(k).wait_recv()
+            spread(0, jnp.sum(ar2[...], axis=0))
+        else:
+            for k in range(len(far)):
+                chip_copy(k).wait_recv()
+            spread(1, jnp.sum(chips[...], axis=0))
+
+    def reduce_drain(cyc):
+        if cyc == 0:
+            for k in range(ngz - 1):
+                line_copy(k).wait_send()
+            for k in range(ngx * ngy - 1):
+                plane_copy(k).wait_send()
+        else:
+            pair_copy().wait_send()
+            for k in range(len(far)):
+                chip_copy(k).wait_send()
 
     def solve(cyc):
         def G(i, j):
@@ -550,6 +601,7 @@
         gacc[1, base + i] = gacc[1, base + i] + eb[NW + i] * (edges - edges_before)
     gacc[1, base + S] = gacc[1, base + S] + (edges * edges - edges_before * edges_before)
     reduce_start(1)
+    reduce_middle(1)
     unpack_edges(last + 1, range(NX))
 
     def first_share(x, carry):
@@ -569,21 +621,14 @@
     drain(NW - 1)
     for v in range(last + 1, NW + S):
         drain(v)
-    for k in range(ngz - 1):
-        line_copy(0, k).wait_send()
-    for k in range(ngx * ngy - 1):
-        plane_copy(0, k).wait_send()
-    reduce_middle(1)
-    for k in range(ngz - 1):
-        line_copy(1, k).wait_send()
+    reduce_drain(0)
     reduce_end(1)
     y, c = solve(1)
     for k in range(S):
         weights_ref[k:k + 1, :] = y[k][0:1]
     for k in range(S + 1):
         weights_ref[8 + k:9 + k, :] = c[k][0:1]
-    for k in range(ngx * ngy - 1):
-        plane_copy(1, k).wait_send()
+    reduce_drain(1)
 
 
 def store(first_ref, basis_ref, weights_ref, sol_hbm, res_hbm, sol, res, sem):
@@ -639,18 +684,23 @@
                 pltpu.VMEM((NV, 6, 8, LANES), f32),
                 pltpu.VMEM((NV, 8, LANES), f32),
                 pltpu.VMEM((2, 16, 8, LANES), f32),
-                pltpu.VMEM((2, ngz, 1, LANES), f32),
-                pltpu.VMEM((2, ngx * ngy, 1, LANES), f32),
+                pltpu.VMEM((ngz, 1, LANES), f32),
+                pltpu.VMEM((ngx * ngy, 1, LANES), f32),
+                pltpu.VMEM((2, 1, LANES), f32),
+                pltpu.VMEM((ngx * ngy * ngz // 2, 1, LANES), f32),
                 pltpu.VMEM((2, 16, LANES), f32),
                 pltpu.VMEM((40, LANES), f32),
                 dma((17,)),
                 pltpu.SemaphoreType.REGULAR((3,)),
                 dma((NV, 14)),
                 dma((NV, 14)),
-                dma((2, ngz - 1)),
-                dma((2, ngz - 1)),
-                dma((2, ngx * ngy - 1)),
-                dma((2, ngx * ngy - 1)),
+                dma((ngz - 1,)),
+                dma((ngz - 1,)),
+                dma((ngx * ngy - 1,)),
+                dma((ngx * ngy - 1,)),
+                dma((2,)),
+                dma((ngx * ngy * ngz // 2 - 1,)),
+                dma((ngx * ngy * ngz // 2 - 1,)),
             ],
             compiler_params=pltpu.CompilerParams(
                 collective_id=0, has_side_effects=True, vmem_limit_bytes=48 << 20

time: 46.9 us -> 46.9 us (level)
  no operation moved by 1% of the time
where the time goes in v6:
time: 46.9 us; the launch traced here: 46.7 us
  Pallas kernels  46.1 us (98%)
  between operations  0.64 us (1%)
    pallas_call x1, Pallas kernels, on_device(): pl.pallas_call(functools.partial(kernel, sizes), out_shape=(out, jax.Shap...  45 us
    pallas_call x1, Pallas kernels, on_device(): pl.pallas_call(store, out_shape=(out, out), in_specs=[pl.BlockSpec(memory...  1.07 us

profile of v6, /device:TPU:1, one launch (start us, length us, event | category | flops | bytes accessed | tf_op | source)
XLA Modules:
  0.0 46.7 jit_solution(13586322384303831979)
XLA Ops:
  0.6 45.0 %gmres.1 = (f32[2,8,32,256]{3,2,1,0:T(8,128)S(1)}, f32[5,2,8,32,256]{4,3,2,1,0:T(8,128)S(1)}, f32[16,128]{1,0:T(8,128)S(1)}) custom-call(bf16[7,4,8,32,256]{4,3,2,1,0:T(8,128)(2,1)} %st_hbm.1, f32[2,8,32,256]{3,2,1,0:T(8,128)} %rs_hbm.1), custom_call_target="tpu_custom_call" | custom-call | tf_op jit(solution)/shard_map/gmres/pallas_call | solution.py:667
  45.7 1.1 %store.1 = (f32[2,8,32,256]{3,2,1,0:T(8,128)}, f32[2,8,32,256]{3,2,1,0:T(8,128)}) custom-call(f32[2,8,32,256]{3,2,1,0:T(8,128)S(1)} %get-tuple-element.5.first_ref, f32[5,2,8,32,256]{4,3,2,1,0:T(8,128)S(1)} %get-tuple-element.6.basis_ref, f32[16,128]{1,0:T(8,128)S(1)} %get-tuple-element.7.weights_ref), custom_call_target="tpu_custom_call" | custom-call | tf_op jit(solution)/shard_map/store/pallas_call | solution.py:714
